TPU v7x, 32 devices: a whole 2x2x4 slice. The times are simulated.
32 devices in a mesh: ctx: 8 (over z, x), shard: 4 (over y, core).
Axes of the slice: x: 2, y: 2, z: 4, core: 2. Of those that a mesh axis runs over, the one named last changes fastest.
Arguments:
- tokens: bfloat16 [8, 512, 2048], P('shard', 'ctx'), may hold values from -6 to 6
- cotangent: bfloat16 [8, 512, 2048], P('shard', 'ctx'), may hold values from -6 to 6
- adapter_index: int32 [8, 1], P('shard'), may hold values from 0 to 7
- w_attn: bfloat16 [4, 2048, 2048], P(None, 'shard'), may hold values from -0.125 to 0.125
- w_gate_up: bfloat16 [2, 2048, 8192], P(None, 'shard'), may hold values from -0.125 to 0.125
- w_down: bfloat16 [8192, 2048], P('shard'), may hold values from -0.0625 to 0.0625
- gains: bfloat16 [4, 2048], P(None, 'shard'), may hold values from 0.5 to 1.5
- a_wide: bfloat16 [6, 8, 16, 2048], P(None, None, None, 'shard'), may hold values from -0.125 to 0.125
- a_down: bfloat16 [8, 16, 8192], P(None, None, 'shard'), may hold values from -0.0625 to 0.0625
- b_model: bfloat16 [5, 8, 16, 2048], P(None, None, None, 'shard'), may hold values from -1.5 to 1.5
- b_hidden: bfloat16 [2, 8, 16, 8192], P(None, None, None, 'shard'), may hold values from -1.5 to 1.5
Outputs:
- output: bfloat16 [8, 512, 2048], P('shard', 'ctx')
- input_grad: float32 [8, 512, 2048], P('shard', 'ctx')
- grad_a_wide: float32 [6, 8, 16, 2048], P(None, None, None, 'shard')
- grad_a_down: float32 [8, 16, 8192], P(None, None, 'shard')
- grad_b_model: float32 [5, 8, 16, 2048], P(None, None, None, 'shard')
- grad_b_hidden: float32 [2, 8, 16, 8192], P(None, None, None, 'shard')
Inputs may be any that keep to these rules, and one draw needn't show every extreme that they name: `adapter_index`: every one of the 8 adapters is the adapter of at least one sequence.
All inputs are finite; a program needn't handle non-finite values.
Results may differ from a plain program's by a relative error of at most 0.025.
Values may be sent and summed in bfloat16 or wider, within the bound.
No kernel may reach another device: no remote copies, remote signals or barrier semaphores. Data moves between devices by JAX's collectives and lax.ppermute only.
A program may use at most 512 MiB of HBM per device.

v0:
```python
import math

import jax
import jax.numpy as jnp
from jax import lax
from jax.sharding import PartitionSpec as P

D = 2048
HEADS = 16
HD = 128
NADAPT = 8
BLOCK = 256


epsilon = 1e-06
rope_base = 500000.0
far_below = -1e30


def rms_norm(value_in, gain_row):
    return (
        value_in
        * lax.rsqrt(jnp.mean(value_in * value_in, axis=-1, keepdims=True) + epsilon)
        * gain_row.astype(jnp.float32)
    )


def rope_tables(positions):
    freqs_rows = jnp.exp(jnp.arange(0, HD, 2, dtype=jnp.float32) * (-math.log(rope_base) / HD))
    angles = positions.astype(jnp.float32)[:, None] * freqs_rows[None, :]
    return (jnp.cos(angles)[:, None, :], jnp.sin(angles)[:, None, :])


def rotate(value_in, cosine_table, sine_table):
    half_width = value_in.shape[-1] // 2
    first_half = value_in[..., :half_width]
    second_half = value_in[..., half_width:]
    return jnp.concatenate(
        [
            first_half * cosine_table - second_half * sine_table,
            second_half * cosine_table + first_half * sine_table,
        ],
        axis=-1,
    )


def project(inputs, weight, down_sel, up_sel):
    base_term = jnp.einsum("spi,io->spo", inputs, weight, preferred_element_type=jnp.float32)
    lowrank = jnp.einsum(
        "spi,sri->spr", inputs, down_sel, preferred_element_type=jnp.float32
    ).astype(jnp.bfloat16)
    return (
        base_term + jnp.einsum("spr,sro->spo", lowrank, up_sel, preferred_element_type=jnp.float32),
        lowrank,
    )


def project_back(grad_output, inputs, weight, down_sel, up_sel, lowrank):
    grad_inputs = jnp.einsum("spo,io->spi", grad_output, weight, preferred_element_type=jnp.float32)
    grad_lowrank = jnp.einsum(
        "spo,sro->spr", grad_output, up_sel, preferred_element_type=jnp.float32
    ).astype(jnp.bfloat16)
    grad_inputs = grad_inputs + jnp.einsum(
        "spr,sri->spi", grad_lowrank, down_sel, preferred_element_type=jnp.float32
    )
    grad_down = jnp.einsum("spr,spi->sri", grad_lowrank, inputs, preferred_element_type=jnp.float32)
    grad_up = jnp.einsum("spr,spo->sro", lowrank, grad_output, preferred_element_type=jnp.float32)
    return (grad_inputs, grad_down, grad_up)


def score_terms(
    query_heads, key_heads, value_heads, grad_heads, log_rows, delta_rows, visible, factor
):
    scores = (
        jnp.einsum("sqhd,skhd->shqk", query_heads, key_heads, preferred_element_type=jnp.float32)
        * factor
    )
    scores = jnp.where(visible, scores, far_below)
    prob_rows = jnp.where(visible, jnp.exp(scores - log_rows[..., None]), 0.0)
    grad_probs = jnp.einsum(
        "sqhd,skhd->shqk", grad_heads, value_heads, preferred_element_type=jnp.float32
    )
    grad_scores = (prob_rows * (grad_probs - delta_rows[..., None])).astype(jnp.bfloat16)
    return (prob_rows, grad_scores)


def attend_forward(queries, key_rows, values, row_block):
    seq_count, row_count = (queries.shape[0], queries.shape[1])
    factor = 1.0 / math.sqrt(HD)
    init_state = (
        jnp.full((seq_count, HEADS, row_count), far_below, jnp.float32),
        jnp.zeros((seq_count, HEADS, row_count), jnp.float32),
        jnp.zeros((seq_count, HEADS, row_count, HD), jnp.float32),
    )
    key_piece = lax.all_gather(key_rows, "ctx", axis=1, tiled=True)
    value_piece = lax.all_gather(values, "ctx", axis=1, tiled=True)
    span_rows = key_piece.shape[1]
    key_block = jnp.arange(span_rows, dtype=jnp.int32) // BLOCK
    visible = key_block[None, :] <= row_block[:, None]

    def absorb_compute(state_now):
        running, total_sum, accum_rows = state_now
        key_heads = key_piece.reshape(seq_count, span_rows, HEADS, HD)
        value_heads = value_piece.reshape(seq_count, span_rows, HEADS, HD)
        scores = (
            jnp.einsum("sqhd,skhd->shqk", queries, key_heads, preferred_element_type=jnp.float32)
            * factor
        )
        scores = jnp.where(visible, scores, far_below)
        newest = jnp.maximum(running, jnp.max(scores, axis=-1))
        weights = jnp.where(visible, jnp.exp(scores - newest[..., None]), 0.0)
        total_sum = jnp.sum(weights, axis=-1)
        update = jnp.einsum(
            "shqk,skhd->shqd",
            weights.astype(jnp.bfloat16),
            value_heads,
            preferred_element_type=jnp.float32,
        )
        return (newest, total_sum, update)

    running, total_sum, accum_rows = lax.cond(
        jnp.int32(0) // BLOCK > row_block[-1],
        lambda state_now: state_now,
        absorb_compute,
        init_state,
    )
    return (accum_rows / total_sum[..., None], running + jnp.log(total_sum))


def on_device(
    tokens,
    cotangent,
    adapter_index,
    w_attn,
    w_gate_up,
    w_down,
    gains,
    a_wide,
    a_down,
    b_model,
    b_hidden,
):
    seq_count, row_count = (tokens.shape[0], tokens.shape[1])
    factor = 1.0 / math.sqrt(HD)
    attention_weights, norm_gains, wide_downs, model_ups = (
        lax.all_gather(w_attn, "shard", axis=1, tiled=True),
        lax.all_gather(gains, "shard", axis=1, tiled=True),
        lax.all_gather(a_wide, "shard", axis=3, tiled=True),
        lax.all_gather(b_model, "shard", axis=3, tiled=True),
    )
    gate_upper, down_weights, down_maps, hidden_ups = (
        lax.all_gather(w_gate_up, "shard", axis=1, tiled=True),
        lax.all_gather(w_down, "shard", axis=0, tiled=True),
        lax.all_gather(a_down, "shard", axis=2, tiled=True),
        lax.all_gather(b_hidden, "shard", axis=3, tiled=True),
    )
    choose = adapter_index[:, 0][:, None] == jnp.arange(NADAPT, dtype=jnp.int32)[None, :]
    choose_low = choose.astype(jnp.bfloat16)

    def pick_rows(table_rows):
        return jnp.einsum(
            "sn,pnrw->psrw", choose_low, table_rows, preferred_element_type=jnp.float32
        ).astype(jnp.bfloat16)

    chosen_wide = pick_rows(wide_downs)
    chosen_model = pick_rows(model_ups)
    chosen_hidden = pick_rows(hidden_ups)
    chosen_down = jnp.einsum(
        "sn,nrw->srw", choose_low, down_maps, preferred_element_type=jnp.float32
    ).astype(jnp.bfloat16)
    positions = lax.axis_index("ctx") * row_count + jnp.arange(row_count, dtype=jnp.int32)
    row_block = positions // BLOCK
    cosine_table, sine_table = rope_tables(positions)

    def query_path(pre_value):
        return rotate(
            rms_norm(pre_value, norm_gains[0]).reshape(seq_count, row_count, HEADS, HD),
            cosine_table,
            sine_table,
        )

    def key_path(pre_value):
        return rotate(
            rms_norm(pre_value, norm_gains[1]).reshape(seq_count, row_count, HEADS, HD),
            cosine_table,
            sine_table,
        )

    query_pre, query_low = project(tokens, attention_weights[0], chosen_wide[0], chosen_model[0])
    key_pre, key_low = project(tokens, attention_weights[1], chosen_wide[1], chosen_model[1])
    value_pre, value_low = project(tokens, attention_weights[2], chosen_wide[2], chosen_model[2])
    queries = query_path(query_pre).astype(jnp.bfloat16)
    key_heads = key_path(key_pre).astype(jnp.bfloat16)
    key_rows = key_heads.reshape(seq_count, row_count, D)
    values = value_pre.astype(jnp.bfloat16)
    mixed_heads, log_rows = attend_forward(queries, key_rows, values, row_block)
    mixed_low = (
        mixed_heads.transpose(0, 2, 1, 3).reshape(seq_count, row_count, D).astype(jnp.bfloat16)
    )
    attention_pre, out_low = project(
        mixed_low, attention_weights[3], chosen_wide[3], chosen_model[3]
    )
    resid_sum = tokens.astype(jnp.float32) + rms_norm(attention_pre, norm_gains[2])
    resid_low = resid_sum.astype(jnp.bfloat16)
    gate_pre, gate_low = project(resid_low, gate_upper[0], chosen_wide[4], chosen_hidden[0])
    upper_pre, upper_low = project(resid_low, gate_upper[1], chosen_wide[5], chosen_hidden[1])
    activation = (jax.nn.silu(gate_pre) * upper_pre).astype(jnp.bfloat16)
    feed_pre, feed_low = project(activation, down_weights, chosen_down, chosen_model[4])
    output = (resid_sum + rms_norm(feed_pre, norm_gains[3])).astype(jnp.bfloat16)
    grad_output = cotangent.astype(jnp.float32)
    _, feed_norm_back = jax.vjp(lambda pre_value: rms_norm(pre_value, norm_gains[3]), feed_pre)
    grad_feed = feed_norm_back(grad_output)[0].astype(jnp.bfloat16)
    grad_act, down_grad_a, down_grad_b = project_back(
        grad_feed, activation, down_weights, chosen_down, chosen_model[4], feed_low
    )
    _, swish_back = jax.vjp(
        lambda left_arg, right_arg: jax.nn.silu(left_arg) * right_arg, gate_pre, upper_pre
    )
    grad_gate, grad_upper = swish_back(grad_act)
    gate_in, gate_grad_a, gate_grad_b = project_back(
        grad_gate.astype(jnp.bfloat16),
        resid_low,
        gate_upper[0],
        chosen_wide[4],
        chosen_hidden[0],
        gate_low,
    )
    upper_in, upper_grad_a, upper_grad_b = project_back(
        grad_upper.astype(jnp.bfloat16),
        resid_low,
        gate_upper[1],
        chosen_wide[5],
        chosen_hidden[1],
        upper_low,
    )
    grad_resid = grad_output + gate_in + upper_in
    _, post_norm_back = jax.vjp(lambda pre_value: rms_norm(pre_value, norm_gains[2]), attention_pre)
    grad_attention = post_norm_back(grad_resid)[0].astype(jnp.bfloat16)
    mixed_in, out_grad_a, out_grad_b = project_back(
        grad_attention, mixed_low, attention_weights[3], chosen_wide[3], chosen_model[3], out_low
    )
    grad_mixed = mixed_in.astype(jnp.bfloat16)
    grad_heads = grad_mixed.reshape(seq_count, row_count, HEADS, HD)
    delta_rows = jnp.sum(
        grad_heads.astype(jnp.float32).transpose(0, 2, 1, 3) * mixed_heads, axis=-1
    )
    zero_query = jnp.zeros((seq_count, row_count, HEADS, HD), jnp.float32)
    full_rows = lax.axis_size("ctx") * row_count
    zero_full = jnp.zeros((seq_count, full_rows, D), jnp.float32)
    key_piece = lax.all_gather(key_rows, "ctx", axis=1, tiled=True)
    value_piece = lax.all_gather(values, "ctx", axis=1, tiled=True)
    span_rows = key_piece.shape[1]
    key_block = jnp.arange(span_rows, dtype=jnp.int32) // BLOCK
    visible = key_block[None, :] <= row_block[:, None]

    def query_compute(state_now):
        piece_keys = key_piece.reshape(seq_count, span_rows, HEADS, HD)
        piece_values = value_piece.reshape(seq_count, span_rows, HEADS, HD)
        prob_rows, grad_scores = score_terms(
            queries, piece_keys, piece_values, grad_heads, log_rows, delta_rows, visible, factor
        )
        grad_query = factor * jnp.einsum(
            "shqk,skhd->sqhd", grad_scores, piece_keys, preferred_element_type=jnp.float32
        )
        key_term = (
            factor
            * jnp.einsum(
                "shqk,sqhd->skhd", grad_scores, queries, preferred_element_type=jnp.float32
            )
        ).reshape(seq_count, span_rows, D)
        value_term = jnp.einsum(
            "shqk,sqhd->skhd",
            prob_rows.astype(jnp.bfloat16),
            grad_heads,
            preferred_element_type=jnp.float32,
        ).reshape(seq_count, span_rows, D)
        return (grad_query, key_term, value_term)

    grad_queries, key_sums, value_sums = lax.cond(
        jnp.int32(0) // BLOCK > row_block[-1],
        lambda state_now: state_now,
        query_compute,
        (zero_query, zero_full, zero_full),
    )
    grad_keys, grad_values = (
        lax.psum_scatter(
            key_sums.astype(jnp.bfloat16), "ctx", scatter_dimension=1, tiled=True
        ).astype(jnp.float32),
        lax.psum_scatter(
            value_sums.astype(jnp.bfloat16), "ctx", scatter_dimension=1, tiled=True
        ).astype(jnp.float32),
    )
    grad_keys = grad_keys.reshape(seq_count, row_count, HEADS, HD)
    _, query_back = jax.vjp(query_path, query_pre)
    grad_query_pre = query_back(grad_queries)[0].astype(jnp.bfloat16)
    _, key_back = jax.vjp(key_path, key_pre)
    grad_key_pre = key_back(grad_keys)[0].astype(jnp.bfloat16)
    grad_value_pre = grad_values.astype(jnp.bfloat16)
    query_in, query_grad_a, query_grad_b = project_back(
        grad_query_pre, tokens, attention_weights[0], chosen_wide[0], chosen_model[0], query_low
    )
    key_in, key_grad_a, key_grad_b = project_back(
        grad_key_pre, tokens, attention_weights[1], chosen_wide[1], chosen_model[1], key_low
    )
    value_in, value_grad_a, value_grad_b = project_back(
        grad_value_pre, tokens, attention_weights[2], chosen_wide[2], chosen_model[2], value_low
    )
    input_grad = grad_resid + query_in + key_in + value_in
    choose_full = choose.astype(jnp.float32)
    wide_stack = jnp.stack(
        [query_grad_a, key_grad_a, value_grad_a, out_grad_a, gate_grad_a, upper_grad_a]
    )
    model_stack = jnp.stack([query_grad_b, key_grad_b, value_grad_b, out_grad_b, down_grad_b])
    hidden_stack = jnp.stack([gate_grad_b, upper_grad_b])
    grad_wide = jnp.einsum(
        "sn,psrw->pnrw", choose_full, wide_stack, precision=lax.Precision.HIGHEST
    )
    grad_down = jnp.einsum("sn,srw->nrw", choose_full, down_grad_a, precision=lax.Precision.HIGHEST)
    grad_model = jnp.einsum(
        "sn,psrw->pnrw", choose_full, model_stack, precision=lax.Precision.HIGHEST
    )
    grad_hidden = jnp.einsum(
        "sn,psrw->pnrw", choose_full, hidden_stack, precision=lax.Precision.HIGHEST
    )
    parted = (
        lax.psum_scatter(
            grad_wide.astype(jnp.bfloat16), "shard", scatter_dimension=3, tiled=True
        ).astype(jnp.float32),
        lax.psum_scatter(
            grad_down.astype(jnp.bfloat16), "shard", scatter_dimension=2, tiled=True
        ).astype(jnp.float32),
        lax.psum_scatter(
            grad_model.astype(jnp.bfloat16), "shard", scatter_dimension=3, tiled=True
        ).astype(jnp.float32),
        lax.psum_scatter(
            grad_hidden.astype(jnp.bfloat16), "shard", scatter_dimension=3, tiled=True
        ).astype(jnp.float32),
    )
    result_rows = (
        lax.psum(parted[0].astype(jnp.bfloat16), "ctx").astype(jnp.float32),
        lax.psum(parted[1].astype(jnp.bfloat16), "ctx").astype(jnp.float32),
        lax.psum(parted[2].astype(jnp.bfloat16), "ctx").astype(jnp.float32),
        lax.psum(parted[3].astype(jnp.bfloat16), "ctx").astype(jnp.float32),
    )
    return (output, input_grad, result_rows[0], result_rows[1], result_rows[2], result_rows[3])


def solution(mesh):
    return jax.shard_map(
        on_device,
        mesh=mesh,
        in_specs=(
            P("shard", "ctx", None),
            P("shard", "ctx", None),
            P("shard", None),
            P(None, "shard", None),
            P(None, "shard", None),
            P("shard", None),
            P(None, "shard"),
            P(None, None, None, "shard"),
            P(None, None, "shard"),
            P(None, None, None, "shard"),
            P(None, None, None, "shard"),
        ),
        out_specs=(
            P("shard", "ctx", None),
            P("shard", "ctx", None),
            P(None, None, None, "shard"),
            P(None, None, "shard"),
            P(None, None, None, "shard"),
            P(None, None, None, "shard"),
        ),
        check_vma=False,
    )
```

profile of v0, /device:TPU:0, one launch (start us, length us, event | category | flops | bytes accessed | tf_op | source)
XLA Modules:
  0.0 1789.8 jit_solution(16103788429341072485)
XLA Ops:
  15.9 22.5 %all-gather.14.cloned.1.call-done = bf16[5,8,16,2048]{3,1,2,0:T(8,128)(2,1)} async-done(((bf16[5,8,16,512]{3,1,2,0:T(8,128)(2,1)}), bf16[5,8,16,2048]{3,1,2,0:T(8,128)(2,1)}) %all-gather.14.cloned.1.call-update) | async-done | bytes 2621456 | tf_op jit(solution)/shard_map/all_gather | solution.py:149
  42.2 26.9 %all-gather.12.cloned.1.call-done = bf16[6,8,16,2048]{3,1,2,0:T(8,128)(2,1)} async-done(((bf16[6,8,16,512]{3,1,2,0:T(8,128)(2,1)}), bf16[6,8,16,2048]{3,1,2,0:T(8,128)(2,1)}) %all-gather.12.cloned.1.call-update) | async-done | bytes 3145744 | tf_op jit(solution)/shard_map/all_gather | solution.py:148
  73.1 199.2 %all-gather.10.cloned.1.call-done = bf16[4,2048,2048]{2,1,0:T(8,128)(2,1)} async-done(((bf16[4,512,2048]{2,1,0:T(8,128)(2,1)}), bf16[4,2048,2048]{2,1,0:T(8,128)(2,1)}) %all-gather.10.cloned.1.call-update) | async-done | bytes 33554448 | tf_op jit(solution)/shard_map/all_gather | solution.py:146
  306.1 27.3 %all-gather.22.cloned.1.call-done = bf16[2,8,16,8192]{3,1,2,0:T(8,128)(2,1)} async-done(((bf16[2,8,16,2048]{3,1,2,0:T(8,128)(2,1)}), bf16[2,8,16,8192]{3,1,2,0:T(8,128)(2,1)}) %all-gather.22.cloned.1.call-update) | async-done | bytes 4194320 | tf_op jit(solution)/shard_map/all_gather | solution.py:155
  339.7 69.7 %all-gather.18.cloned.1.call-done = bf16[2,512,2048]{2,1,0:T(8,128)(2,1)} async-done(((bf16[2,64,2048]{2,1,0:T(8,128)(2,1)}), bf16[2,512,2048]{2,1,0:T(8,128)(2,1)}) %all-gather.18.cloned.1.call-update) | async-done | bytes 4194320 | tf_op jit(solution)/shard_map/all_gather | solution.py:96
  409.4 74.4 %all-gather.16.cloned.1.call-done = bf16[2,512,2048]{2,1,0:T(8,128)(2,1)} async-done(((bf16[2,64,2048]{2,1,0:T(8,128)(2,1)}), bf16[2,512,2048]{2,1,0:T(8,128)(2,1)}) %all-gather.16.cloned.1.call-update) | async-done | bytes 4194320 | tf_op jit(solution)/shard_map/all_gather | solution.py:95
  493.1 7.7 fusion.71
  503.5 372.9 %all-gather.20.cloned.1.call-done = bf16[2,2048,8192]{2,1,0:T(8,128)(2,1)} async-done(((bf16[2,512,8192]{2,1,0:T(8,128)(2,1)}), bf16[2,2048,8192]{2,1,0:T(8,128)(2,1)}) %all-gather.20.cloned.1.call-update) | async-done | bytes 67108880 | tf_op jit(solution)/shard_map/all_gather | solution.py:152
  876.4 18.6 %fusion.56 = f32[2,64,8192]{2,1,0:T(8,128)} fusion(bf16[2,64,2048]{2,1,0:T(8,128)(2,1)S(1)} %fusion.110, bf16[2,2048,8192]{2,1,0:T(8,128)(2,1)} %all-gather.20.cloned.1.call-done), kind=kOutput, calls=%fused_computation.57 | convolution fusion | flops 4294967296 | bytes 38273024 | tf_op jit(solution)/shard_map/spi,io->spo/dot_general | solution.py:48
  901.8 16.6 fusion.58
  918.4 7.9 multiply_convert_fusion.2
  927.5 152.1 %all-gather.24.cloned.1.call-done = bf16[8192,2048]{1,0:T(8,128)(2,1)} async-done(((bf16[2048,2048]{1,0:T(8,128)(2,1)}), bf16[8192,2048]{1,0:T(8,128)(2,1)}) %all-gather.24.cloned.1.call-update) | async-done | bytes 33554448 | tf_op jit(solution)/shard_map/all_gather | solution.py:153
  1079.6 13.0 fusion.53
  1098.4 21.0 %fusion.74 = (bf16[2,64,8192]{2,1,0:T(8,128)(2,1)}, bf16[2,64,8192]{2,1,0:T(8,128)(2,1)}) fusion(f32[2,64,8192]{2,1,0:T(8,128)} %convolution_add_fusion.1, f32[2,64,8192]{2,1,0:T(8,128)} %get-tuple-element.224, f32[2,64,8192]{2,1,0:T(8,128)} %fusion.114, bf16[2,64,2048]{2,1,0:T(8,128)(2,1)} %copy-done.17, bf16[8192,2048]{1,0:T(8,128)(2,1)} %all-gather.24.cloned.1.call-done), kind=kOutput, calls=%fused_computation.86 | convolution fusion | flops 4310695936 | bytes 50855936 | tf_op jit(solution)/shard_map/spo,io->spi/dot_general | solution.py:59
  1124.2 16.7 fusion.57
  1143.4 17.0 fusion.55
  1173.1 18.5 %conditional.3 = (bf16[2,512,2048]{1,2,0:T(8,128)(2,1)}, bf16[2,512,2048]{1,2,0:T(8,128)(2,1)}, f32[2,64,16,64]{3,1,2,0:T(8,128)}, f32[2,64,16,64]{3,2,1,0:T(8,128)}, f32[2,64,16,64]{3,2,1,0:T(8,128)}) conditional(s32[]{:T(128)} %bitcast.5, (pred[64,512]{1,0:T(8,128)(4,1)S(1)}, bf16[2,512,2048]{2,1,0:T(8,128)(2,1)S(1)}, ...), branch_computations={%region_10.12_spmd, %region_12.13_spmd} | conditional | flops 1359872000 | bytes 49930280 | solution.py:279
  1191.6 11.4 copy.231
  1203.0 11.4 copy.235
  1230.3 255.3 %all-reduce.13.cloned.1.call-done = (bf16[2,512,2048]{2,0,1:T(2,128)(2,1)}, bf16[2,512,2048]{2,0,1:T(2,128)(2,1)}) async-done(((bf16[2,512,2048]{2,0,1:T(2,128)(2,1)}, bf16[2,512,2048]{2,0,1:T(2,128)(2,1)}), (bf16[2,512,2048]{2,0,1:T(2,128)(2,1)}, bf16[2,512,2048]{2,0,1:T(2,128)(2,1)})) %all-reduce.13.cloned.1.call-update) | async-done | bytes 8388624
  1518.7 47.1 %reduce-scatter.11.cloned.1.call-done = bf16[2,8,16,2048]{3,1,2,0:T(8,128)(2,1)} async-done(((bf16[2,8,16,8192]{3,1,2,0:T(8,128)(2,1)}), bf16[2,8,16,2048]{3,1,2,0:T(8,128)(2,1)}) %reduce-scatter.11.cloned.1.call-update) | async-done | bytes 1048592 | tf_op jit(solution)/shard_map/reduce_scatter | solution.py:335
  1565.8 37.2 %reduce-scatter.9.cloned.1.call-done = bf16[5,8,16,512]{3,1,2,0:T(8,128)(2,1)} async-done(((bf16[5,8,16,2048]{3,1,2,0:T(8,128)(2,1)}), bf16[5,8,16,512]{3,1,2,0:T(8,128)(2,1)}) %reduce-scatter.9.cloned.1.call-update) | async-done | bytes 655376 | tf_op jit(solution)/shard_map/reduce_scatter | solution.py:332
  1603.0 40.5 %reduce-scatter.5.cloned.1.call-done = bf16[6,8,16,512]{3,1,2,0:T(8,128)(2,1)} async-done(((bf16[6,8,16,2048]{3,1,2,0:T(8,128)(2,1)}), bf16[6,8,16,512]{3,1,2,0:T(8,128)(2,1)}) %reduce-scatter.5.cloned.1.call-update) | async-done | bytes 786448 | tf_op jit(solution)/shard_map/reduce_scatter | solution.py:326
  1665.4 109.4 %all-reduce.11.cloned.1.call-done = (bf16[6,8,16,512]{3,1,2,0:T(8,128)(2,1)}, bf16[8,16,2048]{2,0,1:T(8,128)(2,1)}, bf16[5,8,16,512]{3,1,2,0:T(8,128)(2,1)}, bf16[2,8,16,2048]{3,1,2,0:T(8,128)(2,1)}) async-done(((bf16[6,8,16,512]{3,1,2,0:T(8,128)(2,1)}, bf16[8,16,2048]{2,0,1:T(8,128)(2,1)}, bf16[5,8,16,512]{3,1,2,0:T(8,128)(2,1)}, bf16[2,8,16,2048]{3,1,2,0:T(8,128)(2,1)}), ...) | async-done | bytes 3014672 | tf_op jit(solution)/shard_map/psum | solution.py:340
  (383 shorter events, 204.3 us)
Async XLA Ops:
  7.2 31.3 %all-gather.14.cloned.1.call-start = ((), (), s32[]{:S(2)}) async-start(), calls=%async_computation.6 | async-start | bytes 3276800 | tf_op jit(solution)/shard_map/all_gather | solution.py:149
  9.5 59.6 %all-gather.12.cloned.1.call-start = ((), (), s32[]{:S(2)}) async-start(), calls=%async_computation.5 | async-start | bytes 3932160 | tf_op jit(solution)/shard_map/all_gather | solution.py:148
  12.1 260.2 %all-gather.10.cloned.1.call-start = ((), (), s32[]{:S(2)}) async-start(), calls=%async_computation.4 | async-start | bytes 41943040 | tf_op jit(solution)/shard_map/all_gather | solution.py:146
  12.8 290.1 %all-gather.26.cloned.1.call-start = ((), (), s32[]{:S(2)}) async-start(), calls=%async_computation.12 | async-start | bytes 2621440 | tf_op jit(solution)/shard_map/all_gather | solution.py:154
  14.2 319.2 %all-gather.22.cloned.1.call-start = ((), (), s32[]{:S(2)}) async-start(), calls=%async_computation.10 | async-start | bytes 5242880 | tf_op jit(solution)/shard_map/all_gather | solution.py:155
  15.9 393.6 %all-gather.18.cloned.1.call-start = ((), (), s32[]{:S(2)}) async-start(), calls=%async_computation.8 | async-start | bytes 4718592 | tf_op jit(solution)/shard_map/all_gather | solution.py:96
  42.2 247.4 %copy-start.39 = (bf16[2,16,2048]{2,0,1:T(2,128)(2,1)}, bf16[2,16,2048]{2,0,1:T(2,128)(2,1)S(1)}, u32[]{:S(2)}) copy-start(bf16[2,16,2048]{2,0,1:T(2,128)(2,1)S(1)} %get-tuple-element.203) | copy-start | bytes 393220
  42.2 253.9 %copy-start.37 = (bf16[2,16,2048]{2,0,1:T(2,128)(2,1)}, bf16[2,16,2048]{2,0,1:T(2,128)(2,1)S(1)}, u32[]{:S(2)}) copy-start(bf16[2,16,2048]{2,0,1:T(2,128)(2,1)S(1)} %get-tuple-element.204) | copy-start | bytes 393220
  72.8 420.0 %copy-start.50 = (bf16[2,16,2048]{2,0,1:T(2,128)(2,1)}, bf16[2,16,2048]{2,0,1:T(2,128)(2,1)S(1)}, u32[]{:S(2)}) copy-start(bf16[2,16,2048]{2,0,1:T(2,128)(2,1)S(1)} %get-tuple-element.196) | copy-start | bytes 393220
  278.1 205.8 %all-gather.16.cloned.1.call-start = ((), (), s32[]{:S(2)}) async-start(), calls=%async_computation.7 | async-start | bytes 4718592 | tf_op jit(solution)/shard_map/all_gather | solution.py:95
  300.0 576.4 %all-gather.20.cloned.1.call-start = ((), (), s32[]{:S(2)}) async-start(), calls=%async_computation.9 | async-start | bytes 83886080 | tf_op jit(solution)/shard_map/all_gather | solution.py:152
  300.8 778.8 %all-gather.24.cloned.1.call-start = ((), (), s32[]{:S(2)}) async-start(), calls=%async_computation.11 | async-start | bytes 41943040 | tf_op jit(solution)/shard_map/all_gather | solution.py:153
  301.5 1184.1 %all-reduce.13.cloned.1.call-start = ((), (), s32[]{:S(2)}) async-start(), calls=%async_computation.18 | async-start | bytes 16777216
  338.6 556.5 %copy-start.21 = (bf16[2,16,8192]{2,0,1:T(2,128)(2,1)}, bf16[2,16,8192]{2,0,1:T(2,128)(2,1)S(1)}, u32[]{:S(2)}) copy-start(bf16[2,16,8192]{2,0,1:T(2,128)(2,1)S(1)} %get-tuple-element.192) | copy-start | bytes 1572868
  501.3 393.8 %copy-start.106 = (f32[2,64]{1,0:T(2,128)}, f32[2,64]{1,0:T(2,128)S(1)}, u32[]{:S(2)}) copy-start(f32[2,64]{1,0:T(2,128)S(1)} %get-tuple-element.221) | copy-start | bytes 1540
  501.3 393.8 %copy-start.100 = (f32[2,64]{1,0:T(2,128)}, f32[2,64]{1,0:T(2,128)S(1)}, u32[]{:S(2)}) copy-start(f32[2,64]{1,0:T(2,128)S(1)} %fusion.162) | copy-start | bytes 1540
  503.5 391.5 %copy-start.80 = (bf16[2,64,16]{1,2,0:T(8,128)(2,1)}, bf16[2,64,16]{1,2,0:T(8,128)(2,1)S(1)}, u32[]{:S(2)}) copy-start(bf16[2,64,16]{1,2,0:T(8,128)(2,1)S(1)} %convolution_convert_fusion.14) | copy-start | bytes 12292
  1214.4 304.3 %reduce-scatter.7.cloned.1.call-start = ((), (), s32[]{:S(2)}) async-start(), calls=%async_computation.14 | async-start | bytes 2621440 | tf_op jit(solution)/shard_map/reduce_scatter | solution.py:329
  1219.7 346.1 %reduce-scatter.11.cloned.1.call-start = ((), (), s32[]{:S(2)}) async-start(), calls=%async_computation.16 | async-start | bytes 5242880 | tf_op jit(solution)/shard_map/reduce_scatter | solution.py:335
  1229.0 259.8 %copy-start.53 = (f32[64,64]{1,0:T(8,128)S(1)}, f32[64,64]{1,0:T(8,128)}, u32[]{:S(2)}) copy-start(f32[64,64]{1,0:T(8,128)} %copy-done.52) | copy-start | bytes 49156
  1229.0 259.8 %copy-start.55 = (f32[64,64]{1,0:T(8,128)S(1)}, f32[64,64]{1,0:T(8,128)}, u32[]{:S(2)}) copy-start(f32[64,64]{1,0:T(8,128)} %copy-done.54) | copy-start | bytes 49156
  1229.0 374.0 %reduce-scatter.9.cloned.1.call-start = ((), (), s32[]{:S(2)}) async-start(), calls=%async_computation.15 | async-start | bytes 3276800 | tf_op jit(solution)/shard_map/reduce_scatter | solution.py:332
  1509.5 134.1 %reduce-scatter.5.cloned.1.call-start = ((), (), s32[]{:S(2)}) async-start(), calls=%async_computation.13 | async-start | bytes 3932160 | tf_op jit(solution)/shard_map/reduce_scatter | solution.py:326
  1516.6 258.2 %all-reduce.11.cloned.1.call-start = ((), (), s32[]{:S(2)}) async-start(), calls=%async_computation.17 | async-start | bytes 6029312 | tf_op jit(solution)/shard_map/psum | solution.py:340
  (103 other events, 2296.4 us)
Sparse Core Ops, SparseCore 0:
  10.1 28.2 all-gather.13
  40.6 28.5 all-gather.11
  70.7 201.5 all-gather.9
  274.3 22.6 all-gather.25
  298.9 34.4 all-gather.21
  336.0 73.3 all-gather.17
  412.2 71.6 all-gather.15
  485.4 390.9 all-gather.19
  878.0 201.5 all-gather.23
  1214.5 271.0 all-reduce.12
  1488.2 30.4 reduce-scatter.6
  1521.2 44.5 reduce-scatter.10
  1568.3 34.6 reduce-scatter.8
  1605.6 37.9 reduce-scatter.4
  1647.5 127.2 all-reduce.10
where the time goes:
time: 1800 us; the launch traced here: 1790 us
  waiting for transfers between devices  1440 us (80%)
  matrix products  245 us (14%)
  local copies, waits for them, and re-layouts  61.4 us (3%)
  other arithmetic  21.1 us (1%)
    all_gather x1, waiting for transfers between devices, on_device(): lax.all_gather(w_gate_up, 'shard', axis=1, tiled=True)  373 us
    unnamed x16, waiting for transfers between devices  258 us
    all_gather x1, waiting for transfers between devices, on_device(): lax.all_gather(w_attn, 'shard', axis=1, tiled=True)  199 us
    all_gather x1, waiting for transfers between devices, on_device(): lax.all_gather(w_down, 'shard', axis=0, tiled=True)  152 us
    psum x1, waiting for transfers between devices, on_device(): lax.psum(parted[0].astype(jnp.bfloat16), 'ctx').astype(jnp.float32)  109 us
    dot_general x7, matrix products, project_back(): jnp.einsum('spo,io->spi', grad_output, weight, preferred_element_type=jnp...  80.6 us
    all_gather x1, waiting for transfers between devices, attend_forward(): key_piece = lax.all_gather(key_rows, 'ctx', axis=1, tiled=True)  74.4 us
    dot_general x7, matrix products, project(): jnp.einsum('spi,io->spo', inputs, weight, preferred_element_type=jnp.floa...  69.9 us
  transfers between devices with their start and end apart: 15, of which 14 were waited for; matrix products, arithmetic and copies ran while one was open for 10% of the time, Pallas kernels for 0%

commit v1 on v0

v1 whole, which is shorter than its diff:
```python
import math

import jax
import jax.numpy as jnp
from jax import lax
from jax.sharding import PartitionSpec as P

D = 2048
HEADS = 16
HD = 128
BLOCK = 256
CHUNKS = 1

epsilon = 1e-06
rope_base = 500000.0
far_below = -1e30
BF = jnp.bfloat16
F32 = jnp.float32


def dot(left, right):
    return lax.dot_general(left, right, (((1,), (0,)), ((), ())), preferred_element_type=F32)


def dot_nt(left, right):
    return lax.dot_general(left, right, (((1,), (1,)), ((), ())), preferred_element_type=F32)


def dot_tn(left, right):
    return lax.dot_general(left, right, (((0,), (0,)), ((), ())), preferred_element_type=F32)


def over_shard(value, flip):
    size = lax.axis_size("shard")
    return lax.ppermute(value, "shard", [(i, i ^ flip) for i in range(size)])


def over_ctx(value, flip):
    size = lax.axis_size("ctx")
    return lax.ppermute(value, "ctx", [(i, i ^ flip) for i in range(size)])


FLIPS = (0, 2, 1, 3)


def gather_rows(own):
    pair = jnp.concatenate([own, over_shard(own, 2)], axis=0)
    return jnp.concatenate([pair, over_shard(pair, 1)], axis=0)


def scatter_rows(partial):
    rows = partial.shape[0] // 4
    got = over_shard(partial[2 * rows :].astype(BF), 1)
    half = partial[: 2 * rows] + got.astype(F32)
    got = over_shard(half[rows:].astype(BF), 2)
    return half[:rows] + got.astype(F32)


def column_block(value, index, width):
    return lax.dynamic_slice_in_dim(value, index * width, width, value.ndim - 1)


def scatter_columns(partial, shard):
    width = partial.shape[-1] // 4
    blocks = [column_block(partial, shard ^ flip, width) for flip in FLIPS]
    got = over_shard(jnp.stack(blocks[2:]).astype(BF), 1).astype(F32)
    far = (blocks[1] + got[1]).astype(BF)
    return blocks[0] + got[0] + over_shard(far, 2).astype(F32)


def natural(parts, shard):
    out = []
    for index in range(4):
        value = parts[0]
        for flip, part in zip(FLIPS[1:], parts[1:]):
            value = jnp.where((shard ^ flip) == index, part, value)
        out.append(value)
    return out


def relayout(weight, shard, quarter):
    count, depth, full = weight.shape
    width = full // 4
    slim = depth // 4
    mine = lax.dynamic_slice_in_dim(weight, quarter * slim, slim, 1)
    to_far = jnp.stack([column_block(mine, shard ^ 2, width), column_block(mine, shard ^ 3, width)])
    arrived = over_shard(to_far, 2)
    crossed = over_shard(arrived[1], 1)
    held = jnp.stack([arrived[0], crossed])
    from_x = over_ctx(held, 1)
    from_z = over_ctx(held, 2)
    diag_a = over_ctx(from_z[0], 1)
    diag_b = over_ctx(from_x[1], 2)
    near = over_shard(column_block(weight, shard ^ 1, width), 1)
    own = column_block(weight, shard, width)
    whole = jnp.zeros((count, 4 * depth, width), weight.dtype)

    def put(whole, piece, block, part):
        return lax.dynamic_update_slice(
            whole, piece, (jnp.int32(0), block * depth + part * slim, jnp.int32(0))
        )

    zero = jnp.int32(0)
    whole = put(whole, own, shard, zero)
    whole = put(whole, near, shard ^ 1, zero)
    for place, flip in enumerate((2, 3)):
        whole = put(whole, held[place], shard ^ flip, quarter)
        whole = put(whole, from_x[place], shard ^ flip, quarter ^ 1)
        whole = put(whole, from_z[place], shard ^ flip, quarter ^ 2)
    whole = put(whole, diag_a, shard ^ 2, quarter ^ 3)
    whole = put(whole, diag_b, shard ^ 3, quarter ^ 3)
    return whole


def rms_scale(value):
    return lax.rsqrt(jnp.mean(value * value, axis=-1, keepdims=True) + epsilon)


def rms_back(value, scale, gain, grad):
    weighted = grad * gain
    return scale * weighted - value * (
        scale * scale * scale * jnp.mean(value * weighted, axis=-1, keepdims=True)
    )


def rotate(value, cosine, sine):
    half = value.shape[-1] // 2
    first, second = value[..., :half], value[..., half:]
    return jnp.concatenate([first * cosine - second * sine, second * cosine + first * sine], axis=-1)


def group_of(sequence, part, per_sequence, ctx_size):
    if per_sequence > 1:
        return sequence * per_sequence + part
    depth = sequence % (ctx_size // 2)
    return 2 * depth + (depth + sequence // (ctx_size // 2)) % 2


def on_device(
    tokens,
    cotangent,
    adapter_index,
    w_attn,
    w_gate_up,
    w_down,
    gains,
    a_wide,
    a_down,
    b_model,
    b_hidden,
):
    seqs, rows = tokens.shape[0], tokens.shape[1]
    shards, ctxs = lax.axis_size("shard"), lax.axis_size("ctx")
    shard, ctx = lax.axis_index("shard"), lax.axis_index("ctx")
    batch = seqs * shards
    per_sequence = ctxs // batch
    group_rows = batch * rows
    heads = HEADS // shards
    wide = heads * HD
    adapters = a_down.shape[0]
    rank = a_down.shape[1]
    quarter = ctx % 4

    groups = [[group_of(q, k, per_sequence, ctxs) for k in range(per_sequence)] for q in range(batch)]
    sequence_at, part_at = [0] * ctxs, [0] * ctxs
    for q in range(batch):
        for k in range(per_sequence):
            sequence_at[groups[q][k]] = q
            part_at[groups[q][k]] = k
    my_sequence = jnp.array(sequence_at, jnp.int32)[ctx]
    my_part = jnp.array(part_at, jnp.int32)[ctx]
    my_slot = my_sequence % seqs
    my_spot = (ctx % batch) // shards

    pairs = []
    for p in range(seqs):
        pairs.append([])
        for c in range(ctxs):
            for s in range(shards):
                k, local = c // batch, c % batch
                spot, owner = local // shards, local % shards
                to = groups[seqs * s + (p + spot) % seqs][k]
                pairs[p].append((c * shards + s, to * shards + owner))

    def to_groups(value):
        got = []
        for p in range(seqs):
            sent = lax.dynamic_index_in_dim(value, (p + my_spot) % seqs, 0, keepdims=False)
            got.append(lax.ppermute(sent, ("ctx", "shard"), pairs[p]))
        got = jnp.stack(got)
        return [
            lax.dynamic_index_in_dim(got, (my_slot - h) % seqs, 0, keepdims=False)
            for h in range(seqs)
        ]

    def from_groups(parts):
        stacked = jnp.stack(parts)
        got = []
        for p in range(seqs):
            sent = lax.dynamic_index_in_dim(stacked, (my_slot - p) % seqs, 0, keepdims=False)
            got.append(lax.ppermute(sent, ("ctx", "shard"), [(b, a) for a, b in pairs[p]]))
        got = jnp.stack(got)
        return jnp.stack(
            [
                lax.dynamic_index_in_dim(got, (j - my_spot) % seqs, 0, keepdims=False)
                for j in range(seqs)
            ]
        )

    def chunked(parts):
        if CHUNKS == 1:
            return [jnp.concatenate(parts, axis=0)]
        return parts

    def unchunked(chunks):
        if CHUNKS == 1:
            return [chunks[0][h * rows : (h + 1) * rows] for h in range(seqs)]
        return chunks

    token_rows = chunked(to_groups(tokens))
    index_pair = jnp.stack([adapter_index[:, 0], over_shard(adapter_index[:, 0], 2)])
    index_far = over_shard(index_pair, 1)
    index_all = jnp.concatenate(
        natural([index_pair[0], index_pair[1], index_far[0], index_far[1]], shard)
    )
    my_adapter = index_all[my_sequence]
    own_wide = lax.dynamic_index_in_dim(a_wide, my_adapter, 1, keepdims=False)
    own_down = lax.dynamic_index_in_dim(a_down, my_adapter, 0, keepdims=False)
    own_model = lax.dynamic_index_in_dim(b_model, my_adapter, 1, keepdims=False)
    own_hidden = lax.dynamic_index_in_dim(b_hidden, my_adapter, 1, keepdims=False)
    small = jnp.concatenate(
        [
            own_wide[:3].reshape(3 * rank, wide),
            own_wide[4:].reshape(2 * rank, wide),
            own_model[3:].reshape(2 * rank, wide),
            gains[2:],
        ]
    )
    small_pair = jnp.stack([small, over_shard(small, 2)])
    small_far = over_shard(small_pair, 1)
    small_all = jnp.concatenate(
        natural([small_pair[0], small_pair[1], small_far[0], small_far[1]], shard), axis=1
    )
    qkv_downs = small_all[: 3 * rank]
    gate_downs = small_all[3 * rank : 5 * rank]
    out_up = small_all[5 * rank : 6 * rank]
    feed_up = small_all[6 * rank : 7 * rank]
    attn_gain = small_all[7 * rank : 7 * rank + 1].astype(F32)
    feed_gain = small_all[7 * rank + 1 : 7 * rank + 2].astype(F32)

    w_qkv = relayout(w_attn[:3], shard, quarter)
    w_gate = relayout(w_gate_up[:1], shard, quarter)[0]
    w_up = relayout(w_gate_up[1:], shard, quarter)[0]
    w_out = w_attn[3]

    block_of_row = []
    positions = []
    span = rows * seqs // CHUNKS
    for h in range(CHUNKS):
        place = jnp.arange(span, dtype=jnp.int32)
        spots = h * (seqs // CHUNKS) + place // rows
        inner = place % rows
        for flip in FLIPS:
            positions.append(my_part * group_rows + (spots * shards + (shard ^ flip)) * rows + inner)
    positions = jnp.concatenate(positions)
    freqs = jnp.exp(jnp.arange(0, HD, 2, dtype=F32) * (-math.log(rope_base) / HD))
    angles = positions.astype(F32)[:, None] * freqs[None, :]
    cosine, sine = jnp.cos(angles)[:, None, :], jnp.sin(angles)[:, None, :]

    token_all = [gather_rows(x) for x in token_rows]
    token_full = jnp.concatenate(token_all) if len(token_all) > 1 else token_all[0]
    total_rows = token_full.shape[0]

    qkv_low = dot_nt(token_full, qkv_downs).astype(BF)
    lows = [qkv_low[:, p * rank : (p + 1) * rank] for p in range(3)]
    pre = [dot(token_full, w_qkv[p]) + dot(lows[p], own_model[p]) for p in range(3)]

    def over_all_heads(sums):
        shape = sums.shape
        sums = sums.reshape(shape[0], CHUNKS, 2, 2, -1)
        sums = sums + over_shard(sums, 1)[:, :, ::-1]
        sums = sums + over_shard(sums, 2)[:, :, :, ::-1]
        return sums.reshape(shape)

    squares = over_all_heads(
        jnp.stack([jnp.sum(pre[p] * pre[p], axis=-1) for p in range(2)])
    )
    scales = lax.rsqrt(squares / D + epsilon)[:, :, None]
    head_gain = gains[:2].astype(F32)

    def as_heads(value):
        return value.reshape(total_rows, heads, HD)

    queries, key_rows = [
        rotate(as_heads(pre[p] * scales[p] * head_gain[p]), cosine, sine).astype(BF)
        for p in range(2)
    ]
    values = as_heads(pre[2].astype(BF))

    def over_sequence(value):
        if per_sequence == 1:
            return value
        return lax.all_gather(value, "ctx", axis=0, tiled=True, axis_index_groups=groups)

    key_all, value_all = over_sequence(key_rows), over_sequence(values)
    key_block = over_sequence(positions // BLOCK)
    visible = key_block[None, :] <= (positions // BLOCK)[:, None]
    factor = 1.0 / math.sqrt(HD)
    scores = jnp.einsum("qhd,khd->hqk", queries, key_all, preferred_element_type=F32) * factor
    scores = jnp.where(visible, scores, far_below)
    weights = jnp.exp(scores - jnp.max(scores, axis=-1, keepdims=True))
    probs = weights / jnp.sum(weights, axis=-1, keepdims=True)
    probs_low = probs.astype(BF)
    mixed = jnp.einsum("hqk,khd->qhd", probs_low, value_all, preferred_element_type=F32)
    mixed = mixed.astype(BF).reshape(total_rows, wide)

    chunk_rows = total_rows // CHUNKS

    def chunk_of(value, h):
        return value[h * chunk_rows : (h + 1) * chunk_rows]

    cot_rows = chunked(to_groups(cotangent))
    output_rows, grad_resid_rows, grad_mixed_chunks = [], [], []
    down_a = gate_b = up_b = feed_b = gate_up_a = out_a = out_b = 0.0
    for h in range(CHUNKS):
        mix = chunk_of(mixed, h)
        out_low = dot_nt(mix, own_wide[3]).astype(BF)
        attn_pre = scatter_rows(dot(mix, w_out) + dot(out_low, out_up))
        attn_scale = rms_scale(attn_pre)
        resid = token_rows[h].astype(F32) + attn_pre * attn_scale * attn_gain
        resid_low = gather_rows(resid.astype(BF))
        gate_low = dot_nt(resid_low, gate_downs).astype(BF)
        gate_pre = dot(resid_low, w_gate) + dot(gate_low[:, :rank], own_hidden[0])
        up_pre = dot(resid_low, w_up) + dot(gate_low[:, rank:], own_hidden[1])
        gate_sig = jax.nn.sigmoid(gate_pre)
        activation = (gate_pre * gate_sig * up_pre).astype(BF)
        feed_low = dot_nt(activation, own_down).astype(BF)
        feed_pre = scatter_rows(dot(activation, w_down) + dot(feed_low, feed_up))
        feed_scale = rms_scale(feed_pre)
        output_rows.append((resid + feed_pre * feed_scale * feed_gain).astype(BF))

        cot = cot_rows[h].astype(F32)
        grad_feed = gather_rows(rms_back(feed_pre, feed_scale, feed_gain, cot).astype(BF))
        grad_feed_low = dot_nt(grad_feed, feed_up).astype(BF)
        grad_act = dot_nt(grad_feed, w_down) + dot(grad_feed_low, own_down)
        down_a += dot_tn(grad_feed_low, activation)
        feed_b += dot_tn(feed_low, grad_feed)
        grad_up = (grad_act * gate_pre * gate_sig).astype(BF)
        grad_gate = (
            grad_act * up_pre * gate_sig * (1.0 + gate_pre * (1.0 - gate_sig))
        ).astype(BF)
        gate_b += dot_tn(gate_low[:, :rank], grad_gate)
        up_b += dot_tn(gate_low[:, rank:], grad_up)
        grad_gate_low = jnp.concatenate(
            [dot_nt(grad_gate, own_hidden[0]), dot_nt(grad_up, own_hidden[1])], axis=1
        ).astype(BF)
        gate_up_a += dot_tn(grad_gate_low, resid_low)
        grad_resid = cot + scatter_rows(
            dot_nt(grad_gate, w_gate) + dot_nt(grad_up, w_up) + dot(grad_gate_low, gate_downs)
        )
        grad_resid_rows.append(grad_resid)
        grad_attn = gather_rows(rms_back(attn_pre, attn_scale, attn_gain, grad_resid).astype(BF))
        grad_out_low = dot_nt(grad_attn, out_up).astype(BF)
        out_a += dot_tn(grad_out_low, mix)
        out_b += dot_tn(out_low, grad_attn)
        grad_mixed_chunks.append(
            (dot_nt(grad_attn, w_out) + dot(grad_out_low, own_wide[3])).astype(BF)
        )
    output = from_groups(unchunked(output_rows))
    grad_mixed = jnp.concatenate(grad_mixed_chunks) if CHUNKS > 1 else grad_mixed_chunks[0]
    feed_gate = scatter_columns(jnp.concatenate([feed_b, gate_up_a]), shard)

    grad_heads = as_heads(grad_mixed)
    grad_probs = jnp.einsum("qhd,khd->hqk", grad_heads, value_all, preferred_element_type=F32)
    delta = jnp.sum(probs * grad_probs, axis=-1, keepdims=True)
    grad_scores = (probs * (grad_probs - delta)).astype(BF)
    grad_queries = factor * jnp.einsum(
        "hqk,khd->qhd", grad_scores, key_all, preferred_element_type=F32
    )
    grad_keys = factor * jnp.einsum(
        "hqk,qhd->khd", grad_scores, queries, preferred_element_type=F32
    )
    grad_values = jnp.einsum("hqk,qhd->khd", probs_low, grad_heads, preferred_element_type=F32)
    if per_sequence > 1:
        grad_keys, grad_values = [
            lax.psum_scatter(
                g.astype(BF), "ctx", scatter_dimension=0, tiled=True, axis_index_groups=groups
            ).astype(F32)
            for g in (grad_keys, grad_values)
        ]
    weighted = [
        rotate(g, cosine, -sine).reshape(total_rows, wide) * head_gain[p]
        for p, g in enumerate((grad_queries, grad_keys))
    ]
    inner = over_all_heads(jnp.stack([jnp.sum(weighted[p] * pre[p], axis=-1) for p in range(2)]))
    inner = (inner / D)[:, :, None]
    grad_pre = [
        (scales[p] * weighted[p] - pre[p] * (scales[p] * scales[p] * scales[p] * inner[p])).astype(BF)
        for p in range(2)
    ]
    grad_pre.append(grad_values.reshape(total_rows, wide).astype(BF))

    qkv_b = jnp.concatenate([dot_tn(lows[p], grad_pre[p]) for p in range(3)])
    grad_lows = jnp.concatenate(
        [dot_nt(grad_pre[p], own_model[p]) for p in range(3)], axis=1
    ).astype(BF)
    qkv_out = scatter_columns(jnp.concatenate([dot_tn(grad_lows, token_full), out_b]), shard)
    grad_tokens = dot(grad_lows, qkv_downs)
    for p in range(3):
        grad_tokens += dot_nt(grad_pre[p], w_qkv[p])
    input_rows = [
        grad_resid_rows[h] + scatter_rows(chunk_of(grad_tokens, h)) for h in range(CHUNKS)
    ]
    input_grad = from_groups([x.astype(BF) for x in unchunked(input_rows)]).astype(F32)

    narrow = jnp.concatenate(
        [
            qkv_out[: 3 * rank],
            out_a,
            feed_gate[rank:],
            qkv_b,
            qkv_out[3 * rank :],
            feed_gate[:rank],
        ]
    ).astype(BF)
    broad = jnp.concatenate([down_a, gate_b, up_b]).astype(BF)
    narrow_all = lax.all_gather(narrow, "ctx", axis=0)
    broad_all = lax.all_gather(broad, "ctx", axis=0)
    group_table = jnp.array(groups, jnp.int32)
    sequence_with = jnp.sum(
        jnp.where(
            index_all[None, :] == jnp.arange(adapters, dtype=jnp.int32)[:, None],
            jnp.arange(batch, dtype=jnp.int32)[None, :],
            0,
        ),
        axis=1,
    )

    def by_adapter(gathered):
        out = []
        for n in range(adapters):
            total = 0.0
            for k in range(per_sequence):
                total += lax.dynamic_index_in_dim(
                    gathered, group_table[sequence_with[n], k], 0, keepdims=False
                ).astype(F32)
            out.append(total)
        return jnp.stack(out, axis=0)

    narrow_out = by_adapter(narrow_all).reshape(adapters, 11, rank, wide).transpose(1, 0, 2, 3)
    broad_out = by_adapter(broad_all).reshape(adapters, 3, rank, -1).transpose(1, 0, 2, 3)
    return (
        output,
        input_grad,
        narrow_out[:6],
        broad_out[0],
        narrow_out[6:],
        broad_out[1:],
    )


def solution(mesh):
    return jax.shard_map(
        on_device,
        mesh=mesh,
        in_specs=(
            P("shard", "ctx", None),
            P("shard", "ctx", None),
            P("shard", None),
            P(None, "shard", None),
            P(None, "shard", None),
            P("shard", None),
            P(None, "shard"),
            P(None, None, None, "shard"),
            P(None, None, "shard"),
            P(None, None, None, "shard"),
            P(None, None, None, "shard"),
        ),
        out_specs=(
            P("shard", "ctx", None),
            P("shard", "ctx", None),
            P(None, None, None, "shard"),
            P(None, None, "shard"),
            P(None, None, None, "shard"),
            P(None, None, None, "shard"),
        ),
        check_vma=False,
    )
```

time: 1800 us -> 639 us (0.35)
  waiting for transfers between devices: 1440 us -> 195 us
  matrix products: 245 us -> 133 us
  local copies, waits for them, and re-layouts: 61.4 us -> 131 us
  starting transfers between devices: 1 us -> 64.3 us
  between operations: 16.9 us -> 51.8 us
  other arithmetic: 21.1 us -> 54.3 us
    all_gather x9 -> x2, waiting for transfers between devices: 945 us -> 0.01 us  [the longest x1 0.01 us: on_device(): broad_all = lax.all_gather(broad, 'ctx', axis=0)]
    unnamed x16 -> x2, waiting for transfers between devices: 258 us -> 0.03 us
    ppermute x0 -> x57, waiting for transfers between devices: none -> 195 us  [the longest x37 102 us: over_shard(): return lax.ppermute(value, 'shard', [(i, i ^ flip) for i in range(size)])]
    reduce_scatter x4 -> x0, waiting for transfers between devices: 127 us -> none  [the longest x1 47.1 us: on_device(): lax.psum_scatter(grad_hidden.astype(jnp.bfloat16), 'shard', scatter_dimen...]
    dot_general x71 -> x52, matrix products: 245 us -> 128 us  [the longest x18 61 us: dot_nt(): lax.dot_general(left, right, (((1,), (1,)), ((), ())), preferred_element_...]
    psum x1 -> x0, waiting for transfers between devices: 109 us -> none  [on_device(): lax.psum(parted[0].astype(jnp.bfloat16), 'ctx').astype(jnp.float32)]
    ppermute x0 -> x57, starting transfers between devices: none -> 64.2 us  [the longest x37 29 us: over_shard(): return lax.ppermute(value, 'shard', [(i, i ^ flip) for i in range(size)])]
    dynamic_update_slice x0 -> x29, local copies, waits for them, and re-layouts: none -> 39.2 us  [put(): lax.dynamic_update_slice(whole, piece, (jnp.int32(0), block * depth + par...]
  transfers between devices with their start and end apart: 15 -> 59, of which waited for: 14 -> 27; matrix products, arithmetic and copies ran while one was open for 10% -> 28% of each run, Pallas kernels for 0% -> 0%
where the time goes in v1:
time: 639 us; the launch traced here: 630 us
  waiting for transfers between devices  195 us (31%)
  matrix products  133 us (21%)
  local copies, waits for them, and re-layouts  131 us (21%)
  starting transfers between devices  64.3 us (10%)
  other arithmetic  54.3 us (8%)
  between operations  51.8 us (8%)
    ppermute x37, waiting for transfers between devices, over_shard(): return lax.ppermute(value, 'shard', [(i, i ^ flip) for i in range(size)])  102 us
    dot_general x18, matrix products, dot_nt(): lax.dot_general(left, right, (((1,), (1,)), ((), ())), preferred_element_...  61 us
    ppermute x12, waiting for transfers between devices, over_ctx(): return lax.ppermute(value, 'ctx', [(i, i ^ flip) for i in range(size)])  52.8 us
    dot_general x18, matrix products, dot(): lax.dot_general(left, right, (((1,), (0,)), ((), ())), preferred_element_...  51.6 us
    dynamic_update_slice x29, local copies, waits for them, and re-layouts, put(): lax.dynamic_update_slice(whole, piece, (jnp.int32(0), block * depth + par...  39.2 us
    ppermute x37, starting transfers between devices, over_shard(): return lax.ppermute(value, 'shard', [(i, i ^ flip) for i in range(size)])  29 us
    ppermute x4, waiting for transfers between devices, from_groups(): lax.ppermute(sent, ('ctx', 'shard'), [(b, a) for a, b in pairs[p]])  26.4 us
    unnamed x257, local copies, waits for them, and re-layouts  16.2 us
  transfers between devices with their start and end apart: 59, of which 27 were waited for; matrix products, arithmetic and copies ran while one was open for 28% of the time, Pallas kernels for 0%

profile of v1, /device:TPU:0, one launch (start us, length us, event | category | flops | bytes accessed | tf_op | source)
XLA Modules:
  0.0 629.7 jit_solution(1625019146559014085)
XLA Ops:
  7.3 11.7 %fusion.169 = (bf16[1,512,8192]{2,1,0:T(8,128)(2,1)}, bf16[1,512,8192]{2,1,0:T(8,128)(2,1)}) fusion(bf16[2,512,8192]{2,1,0:T(8,128)(2,1)} %param.18), kind=kLoop, calls=%fused_computation.487 | loop fusion | bytes 33554432 | tf_op jit(solution)/shard_map/slice | solution.py:252
  47.7 4.4 squeeze.336.clone.1
  62.9 6.6 %slice.381 = bf16[3,512,2048]{2,1,0:T(8,128)(2,1)} slice(bf16[4,512,2048]{2,1,0:T(8,128)(2,1)} %param.17), slice={[0:3], [0:512], [0:2048]} | slice | bytes 12582912 | tf_op jit(solution)/shard_map/slice | solution.py:251
  101.7 24.4 %collective-permute-done.2 = bf16[128,2048]{1,0:T(8,128)(2,1)S(1)} collective-permute-done((bf16[128,2048]{1,0:T(8,128)(2,1)S(1)}, bf16[128,2048]{1,0:T(8,128)(2,1)S(1)}, u32[]{:S(2)}, u32[]{:S(2)}) %collective-permute-start.2) | collective-permute-done | bytes 524320 | tf_op jit(solution)/shard_map/ppermute | solution.py:35
  140.7 11.2 %collective-permute-done.7 = bf16[2,3,128,512]{3,2,1,0:T(8,128)(2,1)S(1)} collective-permute-done((bf16[2,3,128,512]{3,2,1,0:T(8,128)(2,1)S(1)}, bf16[2,3,128,512]{3,2,1,0:T(8,128)(2,1)S(1)}, u32[]{:S(2)}, u32[]{:S(2)}) %collective-permute-start.7) | collective-permute-done | bytes 786464 | tf_op jit(solution)/shard_map/ppermute | solution.py:40
  163.8 40.9 %collective-permute-done.9 = bf16[3,128,512]{2,1,0:T(8,128)(2,1)S(1)} collective-permute-done((bf16[3,128,512]{2,1,0:T(8,128)(2,1)S(1)}, bf16[3,128,512]{2,1,0:T(8,128)(2,1)S(1)}, u32[]{:S(2)}, u32[]{:S(2)}) %collective-permute-start.9) | collective-permute-done | bytes 393248 | tf_op jit(solution)/shard_map/ppermute | solution.py:40
  236.9 5.8 fusion.179
  275.5 9.6 %collective-permute-done.18 = bf16[128,2048]{1,0:T(8,128)(2,1)S(1)} collective-permute-done((bf16[128,2048]{1,0:T(8,128)(2,1)S(1)}, bf16[128,2048]{1,0:T(8,128)(2,1)S(1)}, u32[]{:S(2)}, u32[]{:S(2)}) %collective-permute-start.18) | collective-permute-done | bytes 524320 | tf_op jit(solution)/shard_map/ppermute | solution.py:35
  289.6 8.4 %collective-permute-done.19 = bf16[128,2048]{1,0:T(8,128)(2,1)S(1)} collective-permute-done((bf16[128,2048]{1,0:T(8,128)(2,1)S(1)}, bf16[128,2048]{1,0:T(8,128)(2,1)S(1)}, u32[]{:S(2)}, u32[]{:S(2)}) %collective-permute-start.19) | collective-permute-done | bytes 524320 | tf_op jit(solution)/shard_map/ppermute | solution.py:35
  304.1 7.1 %convolution_add_fusion.4 = f32[512,2048]{1,0:T(8,128)S(1)} fusion(f32[512,2048]{1,0:T(8,128)S(1)} %fusion.112, bf16[2048,2048]{1,0:T(8,128)(2,1)} %bitcast_dynamic-update-slice_fusion.10, bf16[256,2048]{1,0:T(8,128)(2,1)S(1)} %collective-permute-done.20, bf16[128,2048]{1,0:T(8,128)(2,1)S(1)} %collective-permute-done.19, bf16[128,2048]{1,0:T(8,128)(2,1)S(1)} %fusion.49), kind=kOutput, calls=%fused_computation.17 | convolution fusion | flops 4302307328 | bytes 18874368 | tf_op jit(solution)/shard_map/dot_general | solution.py:22
  311.3 13.0 %multiply_convert_fusion.3 = (bf16[512,2048]{1,0:T(8,128)(2,1)S(1)}, f32[512,2048]{1,0:T(8,128)}) fusion(f32[512,2048]{1,0:T(8,128)S(1)} %convolution_add_fusion.4, f32[512,2048]{1,0:T(8,128)S(1)} %fusion.115, bf16[2048,2048]{1,0:T(8,128)(2,1)} %bitcast_dynamic-update-slice_fusion.4, bf16[256,2048]{1,0:T(8,128)(2,1)S(1)} %collective-permute-done.20, ...), kind=kOutput, calls=%fused_computation.7 | convolution fusion | flops 4308598784 | bytes 25165824 | tf_op jit(solution)/shard_map/dot_general | solution.py:22
  324.3 4.5 fusion.180
  336.6 5.9 collective-permute-start.40
  342.5 13.1 %collective-permute-done.40 = bf16[64,2048]{1,0:T(8,128)(2,1)S(1)} collective-permute-done((bf16[64,2048]{1,0:T(8,128)(2,1)S(1)}, bf16[64,2048]{1,0:T(8,128)(2,1)S(1)}, u32[]{:S(2)}, u32[]{:S(2)}) %collective-permute-start.40) | collective-permute-done | bytes 262176 | tf_op jit(solution)/shard_map/ppermute | solution.py:189
  362.1 11.6 %collective-permute-done.41 = bf16[128,2048]{1,0:T(8,128)(2,1)S(1)} collective-permute-done((bf16[128,2048]{1,0:T(8,128)(2,1)S(1)}, bf16[128,2048]{1,0:T(8,128)(2,1)S(1)}, u32[]{:S(2)}, u32[]{:S(2)}) %collective-permute-start.41) | collective-permute-done | bytes 524320 | tf_op jit(solution)/shard_map/ppermute | solution.py:35
  383.6 13.8 %multiply_convert_fusion.2 = (bf16[512,2048]{1,0:T(8,128)(2,1)}, bf16[512,2048]{1,0:T(8,128)(2,1)}) fusion(f32[512,2048]{1,0:T(8,128)} %copy-done.115, f32[512,2048]{1,0:T(8,128)} %get-tuple-element.135, f32[512,2048]{1,0:T(8,128)} %fusion.107, bf16[2048,2048]{1,0:T(8,128)(2,1)} %param.19, bf16[256,2048]{1,0:T(8,128)(2,1)} %collective-permute-done.42, ...), kind=kOutput, calls=%fused_computation.6 | convolution fusion | flops 4315938816 | bytes 27262976 | tf_op jit(solution)/shard_map/dot_general | solution.py:26
  399.6 10.8 %fusion.181 = f32[512,2048]{1,0:T(8,128)} fusion(bf16[512,2048]{1,0:T(8,128)(2,1)} %get-tuple-element.11, bf16[2048,2048]{1,0:T(8,128)(2,1)} %bitcast_dynamic-update-slice_fusion.4), kind=kOutput, calls=%fused_computation.499 | convolution fusion | flops 4294967296 | bytes 14680064 | tf_op jit(solution)/shard_map/dot_general | solution.py:26
  412.7 9.3 %add_add_fusion.1 = f32[512,2048]{1,0:T(8,128)S(1)} fusion(f32[512,2048]{1,0:T(8,128)S(1)} %fusion.92, f32[512,2048]{1,0:T(8,128)} %fusion.181, bf16[512,2048]{1,0:T(8,128)(2,1)S(1)} %copy-done.19, bf16[2048,2048]{1,0:T(8,128)(2,1)} %bitcast_dynamic-update-slice_fusion.10), kind=kOutput, calls=%fused_computation.4 | convolution fusion | flops 4297064448 | bytes 23068672 | tf_op jit(solution)/shard_map/dot_general | solution.py:26
  437.5 7.3 %collective-permute-done.44 = bf16[128,2048]{1,0:T(8,128)(2,1)} collective-permute-done((bf16[128,2048]{1,0:T(8,128)(2,1)}, bf16[128,2048]{1,0:T(8,128)(2,1)}, u32[]{:S(2)}, u32[]{:S(2)}) %collective-permute-start.44) | collective-permute-done | bytes 524320 | tf_op jit(solution)/shard_map/ppermute | solution.py:35
  452.6 4.4 collective-permute-start.38
  496.5 8.7 %collective-permute-done.45 = bf16[128,2048]{1,0:T(8,128)(2,1)S(1)} collective-permute-done((bf16[128,2048]{1,0:T(8,128)(2,1)}, bf16[128,2048]{1,0:T(8,128)(2,1)S(1)}, u32[]{:S(2)}, u32[]{:S(2)}) %collective-permute-start.45) | collective-permute-done | bytes 524320 | tf_op jit(solution)/shard_map/ppermute | solution.py:35
  570.6 11.1 %collective-permute-done.50 = bf16[128,2048]{1,0:T(8,128)(2,1)S(1)} collective-permute-done((bf16[128,2048]{1,0:T(8,128)(2,1)S(1)}, bf16[128,2048]{1,0:T(8,128)(2,1)S(1)}, u32[]{:S(2)}, u32[]{:S(2)}) %collective-permute-start.50) | collective-permute-done | bytes 524320 | tf_op jit(solution)/shard_map/ppermute | solution.py:35
  584.1 5.0 collective-permute-start.52
  590.2 26.4 %collective-permute-done.52 = bf16[64,2048]{1,0:T(8,128)(2,1)S(1)} collective-permute-done((bf16[64,2048]{1,0:T(8,128)(2,1)S(1)}, bf16[64,2048]{1,0:T(8,128)(2,1)S(1)}, u32[]{:S(2)}, u32[]{:S(2)}) %collective-permute-start.52) | collective-permute-done | bytes 262176 | tf_op jit(solution)/shard_map/ppermute | solution.py:201
  (575 shorter events, 302.9 us)
Async XLA Ops:
  7.2 499.2 %all-gather.5.cloned.1.call-start = ((), (), s32[]{:S(2)}) async-start(), calls=%async_computation.1 | async-start | bytes 1769472 | tf_op jit(solution)/shard_map/all_gather | solution.py:428
  22.7 104.1 %collective-permute-start.29 = (bf16[2,1,128,2048]{3,2,1,0:T(8,128)(2,1)}, bf16[2,1,128,2048]{3,2,1,0:T(8,128)(2,1)S(1)}, u32[]{:S(2)}, u32[]{:S(2)}) collective-permute-start(bf16[2,1,128,2048]{3,2,1,0:T(8,128)(2,1)} %pad_maximum_fusion.8), channel_id=1, source_target_pairs={{0,2},{1,3},{2,0},{3,1},{4,6},{5,7},{6,4},{7,5},{8,10},{9,11},{10,... | collective-permute-start | bytes 3145736 | tf_op jit(solution)/shard_map/ppermute | solution.py:35
  26.8 100.2 %collective-permute-start.22 = (bf16[2,1,128,2048]{3,2,1,0:T(8,128)(2,1)}, bf16[2,1,128,2048]{3,2,1,0:T(8,128)(2,1)S(1)}, u32[]{:S(2)}, u32[]{:S(2)}) collective-permute-start(bf16[2,1,128,2048]{3,2,1,0:T(8,128)(2,1)} %pad_maximum_fusion.6), channel_id=1, source_target_pairs={{0,2},{1,3},{2,0},{3,1},{4,6},{5,7},{6,4},{7,5},{8,10},{9,11},{10,... | collective-permute-start | bytes 3145736 | tf_op jit(solution)/shard_map/ppermute | solution.py:35
  28.7 67.7 %collective-permute-start = (bf16[64,2048]{1,0:T(8,128)(2,1)}, bf16[64,2048]{1,0:T(8,128)(2,1)}, u32[]{:S(2)}, u32[]{:S(2)}) collective-permute-start(bf16[64,2048]{1,0:T(8,128)(2,1)} %get-tuple-element.77), channel_id=1, source_target_pairs={{0,0},{1,16},{2,4},{3,20},{4,1},{5,17},{6,5},{7,21},{8,2},{9,18},{... | collective-permute-start | bytes 786440 | tf_op jit(solution)/shard_map/ppermute | solution.py:189
  32.3 64.2 %collective-permute-start.1 = (bf16[64,2048]{1,0:T(8,128)(2,1)}, bf16[64,2048]{1,0:T(8,128)(2,1)}, u32[]{:S(2)}, u32[]{:S(2)}) collective-permute-start(bf16[64,2048]{1,0:T(8,128)(2,1)} %get-tuple-element.76), channel_id=1, source_target_pairs={{0,12},{1,28},{2,8},{3,24},{4,13},{5,29},{6,9},{7,25},{8,14},{9,30... | collective-permute-start | bytes 786440 | tf_op jit(solution)/shard_map/ppermute | solution.py:189
  35.8 46.4 %collective-permute-start.11 = (s32[2]{0:T(128)S(1)}, s32[2]{0:T(128)S(1)}, u32[]{:S(2)}, u32[]{:S(2)}) collective-permute-start(s32[2]{0:T(128)S(1)} %bitcast.502), channel_id=1, source_target_pairs={{0,2},{1,3},{2,0},{3,1},{4,6},{5,7},{6,4},{7,5},{8,10},{9,11},{10,... | collective-permute-start | bytes 32 | tf_op jit(solution)/shard_map/ppermute | solution.py:35
  95.8 30.4 %collective-permute-start.5 = (bf16[2,3,128,512]{3,2,1,0:T(8,128)(2,1)S(1)}, bf16[2,3,128,512]{3,2,1,0:T(8,128)(2,1)S(1)}, u32[]{:S(2)}, u32[]{:S(2)}) collective-permute-start(bf16[2,3,128,512]{3,2,1,0:T(8,128)(2,1)S(1)} %pad_maximum_fusion.14), channel_id=1, source_target_pairs={{0,2},{1,3},{2,0},{3,1},{4,6},{5,7},{6,4},{7,5},{8,10},{9,11},{10,... | collective-permute-start | bytes 2359304 | tf_op jit(solution)/shard_map/ppermute | solution.py:35
  96.3 37.6 %collective-permute-start.4 = (bf16[3,512,512]{2,1,0:T(8,128)(2,1)}, bf16[3,512,512]{2,1,0:T(8,128)(2,1)S(1)}, u32[]{:S(2)}, u32[]{:S(2)}) collective-permute-start(bf16[3,512,512]{2,1,0:T(8,128)(2,1)} %get-tuple-element.18), channel_id=1, source_target_pairs={{0,1},{1,0},{2,3},{3,2},{4,5},{5,4},{6,7},{7,6},{8,9},{9,8},{10,11... | collective-permute-start | bytes 4718600 | tf_op jit(solution)/shard_map/ppermute | solution.py:35
  130.2 30.1 %collective-permute-start.21 = (bf16[1,512,2048]{2,1,0:T(8,128)(2,1)S(1)}, bf16[1,512,2048]{2,1,0:T(8,128)(2,1)S(1)}, u32[]{:S(2)}, u32[]{:S(2)}) collective-permute-start(bf16[1,512,2048]{2,1,0:T(8,128)(2,1)S(1)} %copy-done.37), channel_id=1, source_target_pairs={{0,1},{1,0},{2,3},{3,2},{4,5},{5,4},{6,7},{7,6},{8,9},{9,8},{10,11... | collective-permute-start | bytes 6291464 | tf_op jit(solution)/shard_map/ppermute | solution.py:35
  136.2 117.2 %collective-permute-start.31 = (bf16[2,1,128,2048]{3,2,1,0:T(8,128)(2,1)}, bf16[2,1,128,2048]{3,2,1,0:T(8,128)(2,1)}, u32[]{:S(2)}, u32[]{:S(2)}) collective-permute-start(bf16[2,1,128,2048]{3,2,1,0:T(8,128)(2,1)} %pad_maximum_fusion.9), channel_id=1, source_target_pairs={{0,4},{4,0},{8,12},{12,8},{16,20},{20,16},{24,28},{28,24},{1,5},{5... | collective-permute-start | bytes 3145736 | tf_op jit(solution)/shard_map/ppermute | solution.py:40
  151.9 98.5 %collective-permute-start.32 = (bf16[2,1,128,2048]{3,2,1,0:T(8,128)(2,1)}, bf16[2,1,128,2048]{3,2,1,0:T(8,128)(2,1)}, u32[]{:S(2)}, u32[]{:S(2)}) collective-permute-start(bf16[2,1,128,2048]{3,2,1,0:T(8,128)(2,1)} %pad_maximum_fusion.9), channel_id=1, source_target_pairs={{0,8},{4,12},{8,0},{12,4},{16,24},{20,28},{24,16},{28,20},{1,9},{5... | collective-permute-start | bytes 3145736 | tf_op jit(solution)/shard_map/ppermute | solution.py:40
  153.5 103.7 %collective-permute-start.24 = (bf16[2,1,128,2048]{3,2,1,0:T(8,128)(2,1)}, bf16[2,1,128,2048]{3,2,1,0:T(8,128)(2,1)}, u32[]{:S(2)}, u32[]{:S(2)}) collective-permute-start(bf16[2,1,128,2048]{3,2,1,0:T(8,128)(2,1)} %pad_maximum_fusion.7), channel_id=1, source_target_pairs={{0,4},{4,0},{8,12},{12,8},{16,20},{20,16},{24,28},{28,24},{1,5},{5... | collective-permute-start | bytes 3145736 | tf_op jit(solution)/shard_map/ppermute | solution.py:40
  157.5 47.2 %collective-permute-start.9 = (bf16[3,128,512]{2,1,0:T(8,128)(2,1)S(1)}, bf16[3,128,512]{2,1,0:T(8,128)(2,1)S(1)}, u32[]{:S(2)}, u32[]{:S(2)}) collective-permute-start(bf16[3,128,512]{2,1,0:T(8,128)(2,1)S(1)} %slice_bitcast_fusion.32), channel_id=1, source_target_pairs={{0,4},{4,0},{8,12},{12,8},{16,20},{20,16},{24,28},{28,24},{1,5},{5... | collective-permute-start | bytes 1179656 | tf_op jit(solution)/shard_map/ppermute | solution.py:40
  160.3 45.2 %collective-permute-start.10 = (bf16[3,128,512]{2,1,0:T(8,128)(2,1)S(1)}, bf16[3,128,512]{2,1,0:T(8,128)(2,1)S(1)}, u32[]{:S(2)}, u32[]{:S(2)}) collective-permute-start(bf16[3,128,512]{2,1,0:T(8,128)(2,1)S(1)} %slice_bitcast_fusion.31), channel_id=1, source_target_pairs={{0,8},{4,12},{8,0},{12,4},{16,24},{20,28},{24,16},{28,20},{1,9},{5... | collective-permute-start | bytes 1179656 | tf_op jit(solution)/shard_map/ppermute | solution.py:40
  204.7 50.7 %collective-permute-start.25 = (bf16[2,1,128,2048]{3,2,1,0:T(8,128)(2,1)}, bf16[2,1,128,2048]{3,2,1,0:T(8,128)(2,1)}, u32[]{:S(2)}, u32[]{:S(2)}) collective-permute-start(bf16[2,1,128,2048]{3,2,1,0:T(8,128)(2,1)} %pad_maximum_fusion.7), channel_id=1, source_target_pairs={{0,8},{4,12},{8,0},{12,4},{16,24},{20,28},{24,16},{28,20},{1,9},{5... | collective-permute-start | bytes 3145736 | tf_op jit(solution)/shard_map/ppermute | solution.py:40
  251.5 37.2 %collective-permute-start.33 = (bf16[1,128,2048]{2,1,0:T(8,128)(2,1)S(1)}, bf16[1,128,2048]{2,1,0:T(8,128)(2,1)S(1)}, u32[]{:S(2)}, u32[]{:S(2)}) collective-permute-start(bf16[1,128,2048]{2,1,0:T(8,128)(2,1)S(1)} %slice_bitcast_fusion.27), channel_id=1, source_target_pairs={{0,4},{4,0},{8,12},{12,8},{16,20},{20,16},{24,28},{28,24},{1,5},{5... | collective-permute-start | bytes 1572872 | tf_op jit(solution)/shard_map/ppermute | solution.py:40
  254.4 43.8 %collective-permute-start.34 = (bf16[1,128,2048]{2,1,0:T(8,128)(2,1)S(1)}, bf16[1,128,2048]{2,1,0:T(8,128)(2,1)S(1)}, u32[]{:S(2)}, u32[]{:S(2)}) collective-permute-start(bf16[1,128,2048]{2,1,0:T(8,128)(2,1)S(1)} %slice_bitcast_fusion.26), channel_id=1, source_target_pairs={{0,8},{4,12},{8,0},{12,4},{16,24},{20,28},{24,16},{28,20},{1,9},{5... | collective-permute-start | bytes 1572872 | tf_op jit(solution)/shard_map/ppermute | solution.py:40
  256.5 42.5 %collective-permute-start.26 = (bf16[1,128,2048]{2,1,0:T(8,128)(2,1)S(1)}, bf16[1,128,2048]{2,1,0:T(8,128)(2,1)S(1)}, u32[]{:S(2)}, u32[]{:S(2)}) collective-permute-start(bf16[1,128,2048]{2,1,0:T(8,128)(2,1)S(1)} %slice_bitcast_fusion.29), channel_id=1, source_target_pairs={{0,4},{4,0},{8,12},{12,8},{16,20},{20,16},{24,28},{28,24},{1,5},{5... | collective-permute-start | bytes 1572872 | tf_op jit(solution)/shard_map/ppermute | solution.py:40
  258.3 41.6 %collective-permute-start.27 = (bf16[1,128,2048]{2,1,0:T(8,128)(2,1)S(1)}, bf16[1,128,2048]{2,1,0:T(8,128)(2,1)S(1)}, u32[]{:S(2)}, u32[]{:S(2)}) collective-permute-start(bf16[1,128,2048]{2,1,0:T(8,128)(2,1)S(1)} %slice_bitcast_fusion.28), channel_id=1, source_target_pairs={{0,8},{4,12},{8,0},{12,4},{16,24},{20,28},{24,16},{28,20},{1,9},{5... | collective-permute-start | bytes 1572872 | tf_op jit(solution)/shard_map/ppermute | solution.py:40
  433.1 184.8 %all-gather.3.cloned.1.call-start = ((), (), s32[]{:S(2)}) async-start(), calls=%async_computation | async-start | bytes 1622016 | tf_op jit(solution)/shard_map/all_gather | solution.py:427
  437.2 55.1 %collective-permute-start.56 = (bf16[48,512]{1,0:T(8,128)(2,1)}, bf16[48,512]{1,0:T(8,128)(2,1)}, u32[]{:S(2)}, u32[]{:S(2)}) collective-permute-start(bf16[48,512]{1,0:T(8,128)(2,1)} %fusion.97), channel_id=1, source_target_pairs={{0,2},{1,3},{2,0},{3,1},{4,6},{5,7},{6,4},{7,5},{8,10},{9,11},{10,... | collective-permute-start | bytes 147464 | tf_op jit(solution)/shard_map/ppermute | solution.py:35
  451.0 42.8 %collective-permute-start.37 = (bf16[64,2048]{1,0:T(8,128)(2,1)}, bf16[64,2048]{1,0:T(8,128)(2,1)S(1)}, u32[]{:S(2)}, u32[]{:S(2)}) collective-permute-start(bf16[64,2048]{1,0:T(8,128)(2,1)} %get-tuple-element.69), channel_id=1, source_target_pairs={{0,0},{16,1},{4,2},{20,3},{1,4},{17,5},{5,6},{21,7},{2,8},{18,9},{... | collective-permute-start | bytes 786440 | tf_op jit(solution)/shard_map/ppermute | solution.py:201
  452.6 41.2 %collective-permute-start.38 = (bf16[64,2048]{1,0:T(8,128)(2,1)S(1)}, bf16[64,2048]{1,0:T(8,128)(2,1)S(1)}, u32[]{:S(2)}, u32[]{:S(2)}) collective-permute-start(bf16[64,2048]{1,0:T(8,128)(2,1)S(1)} %get-tuple-element.68), channel_id=1, source_target_pairs={{12,0},{28,1},{8,2},{24,3},{13,4},{29,5},{9,6},{25,7},{14,8},{30,9... | collective-permute-start | bytes 786440 | tf_op jit(solution)/shard_map/ppermute | solution.py:201
  584.1 32.5 %collective-permute-start.52 = (bf16[64,2048]{1,0:T(8,128)(2,1)S(1)}, bf16[64,2048]{1,0:T(8,128)(2,1)S(1)}, u32[]{:S(2)}, u32[]{:S(2)}) collective-permute-start(bf16[64,2048]{1,0:T(8,128)(2,1)S(1)} %get-tuple-element.60), channel_id=1, source_target_pairs={{12,0},{28,1},{8,2},{24,3},{13,4},{29,5},{9,6},{25,7},{14,8},{30,9... | collective-permute-start | bytes 786440 | tf_op jit(solution)/shard_map/ppermute | solution.py:201
  (153 other events, 2165.6 us)
Sparse Core Ops, SparseCore 0:
  433.2 53.3 all-gather.4
  564.5 53.0 all-gather.2
